TPU v7x, 32 devices: a whole 2x2x4 slice. The times are simulated.
32 devices in a mesh: section: 4 (over y, x), seq: 8 (over z, core).
Axes of the slice: x: 2, y: 2, z: 4, core: 2. Of those that a mesh axis runs over, the one named last changes fastest.
Arguments:
- tokens: bfloat16 [4, 2048, 4096], P('section', 'seq'), may hold values from -6 to 6
- norm_gain: bfloat16 [4, 4096], P('section'), may hold values from 0.099609375 to 1.8984375
- w_query: bfloat16 [4, 4096, 2048], P('section', 'seq'), may hold values from -0.09375 to 0.09375
- w_key: bfloat16 [4, 4096, 512], P('section', 'seq'), may hold values from -1.903125 to 1.903125
- w_value: bfloat16 [4, 4096, 512], P('section', 'seq'), may hold values from -0.09375 to 0.09375
Outputs:
- received: bfloat16 [4, 2048, 2048], P('section', 'seq')
All inputs are finite; a program needn't handle non-finite values.
Results may differ from a plain program's by a relative error of at most 0.012.
The roundings to bfloat16 on the way count: a program that leaves them out, or rounds other values in their place, can miss the bound.
Values may be sent and summed in bfloat16 or wider, within the bound.
A program may use at most 192 MiB of HBM per device.

v0:
```python
import jax
import jax.numpy as jnp
from jax import lax
from jax.sharding import PartitionSpec as P

LOCAL_QUERY_HEADS = 16
LOCAL_KEY_HEADS = 4
HEAD_SIZE = 128


def shifted(block, axis, distance):
    devices = range(lax.axis_size(axis))
    route = [((i - distance) % len(devices), i) for i in devices]
    return lax.ppermute(block, axis, route)


def normalize(rows_in, gain_row):
    wide = rows_in.astype(jnp.float32)
    scale = lax.rsqrt(jnp.mean(wide * wide, axis=-1, keepdims=True) + 1e-05)
    return (wide * scale * gain_row.astype(jnp.float32)).astype(jnp.bfloat16)


def rotate(matrix, positions):
    row_count = matrix.shape[0]
    head_count = matrix.shape[1] // HEAD_SIZE
    half_dim = HEAD_SIZE // 2
    shaped = matrix.reshape(row_count, head_count, HEAD_SIZE)
    freqs = jnp.power(
        jnp.float32(500000.0), -(jnp.arange(half_dim).astype(jnp.float32) * 2.0 / HEAD_SIZE)
    )
    angles = positions[:, None] * freqs[None, :]
    cosine = jnp.cos(angles)[:, None, :]
    sine_part = jnp.sin(angles)[:, None, :]
    first_half = shaped[:, :, :half_dim]
    second_half = shaped[:, :, half_dim:]
    turned = jnp.concatenate(
        [
            first_half * cosine - second_half * sine_part,
            second_half * cosine + first_half * sine_part,
        ],
        axis=2,
    )
    return turned.reshape(row_count, head_count * HEAD_SIZE)


def expand(matrix):
    row_count = matrix.shape[0]
    kv_count = matrix.shape[1] // HEAD_SIZE
    query_group_count = LOCAL_QUERY_HEADS // LOCAL_KEY_HEADS
    wide = jnp.broadcast_to(
        matrix.reshape(row_count, kv_count, 1, HEAD_SIZE),
        (row_count, kv_count, query_group_count, HEAD_SIZE),
    )
    return wide.reshape(row_count, kv_count * query_group_count * HEAD_SIZE)


def attend(queries, key_rows, value_rows):
    row_count = queries.shape[0]
    head_count = queries.shape[1] // HEAD_SIZE
    block_rows = min(512, row_count)
    key_heads = key_rows.reshape(row_count, head_count, HEAD_SIZE)
    value_heads = value_rows.reshape(row_count, head_count, HEAD_SIZE)
    key_places = jnp.arange(row_count)

    def one_block(block_index):
        first_row = block_index * block_rows
        query_block = lax.dynamic_slice_in_dim(queries, first_row, block_rows, 0).reshape(
            block_rows, head_count, HEAD_SIZE
        )
        scores = jnp.einsum(
            "qhd,khd->hqk", query_block, key_heads, preferred_element_type=jnp.float32
        ) / jnp.sqrt(jnp.float32(HEAD_SIZE))
        query_places = first_row + jnp.arange(block_rows)
        causal = key_places[None, :] <= query_places[:, None]
        scores = jnp.where(causal[None, :, :], scores, -jnp.inf)
        maxima = jnp.max(scores, axis=-1, keepdims=True)
        expon = jnp.exp(scores - maxima)
        probs = (expon / jnp.sum(expon, axis=-1, keepdims=True)).astype(jnp.bfloat16)
        mixed = jnp.einsum("hqk,khd->qhd", probs, value_heads, preferred_element_type=jnp.float32)
        return mixed.astype(jnp.bfloat16).reshape(block_rows, head_count * HEAD_SIZE)

    blocks = lax.map(one_block, jnp.arange(row_count // block_rows))
    return blocks.reshape(row_count, head_count * HEAD_SIZE)


def per_device(tokens, norm_gain, w_query, w_key, w_value):
    normed = normalize(tokens[0], norm_gain[0])
    query_weight = w_query[0]
    key_weight = w_key[0]
    value_weight = w_value[0]
    query_cols, key_cols, value_cols = (
        lax.all_to_all(query_weight, "seq", split_axis=1, concat_axis=0, tiled=True),
        lax.all_to_all(expand(key_weight), "seq", split_axis=1, concat_axis=0, tiled=True),
        lax.all_to_all(expand(value_weight), "seq", split_axis=1, concat_axis=0, tiled=True),
    )
    gathered = lax.all_gather(normed, "seq", axis=0, tiled=True)
    positions = jnp.arange(gathered.shape[0]).astype(jnp.float32)
    head_queries = rotate(
        jnp.dot(gathered, query_cols, preferred_element_type=jnp.float32), positions
    ).astype(jnp.bfloat16)
    head_keys = rotate(
        jnp.dot(gathered, key_cols, preferred_element_type=jnp.float32), positions
    ).astype(jnp.bfloat16)
    head_values = jnp.dot(gathered, value_cols, preferred_element_type=jnp.float32).astype(
        jnp.bfloat16
    )
    attended = attend(head_queries, head_keys, head_values)
    token_layout = lax.all_to_all(attended, "seq", split_axis=0, concat_axis=1, tiled=True)
    arrived = shifted(token_layout, "section", 1)
    return arrived[None]


def solution(mesh):
    return jax.shard_map(
        per_device,
        mesh=mesh,
        in_specs=(
            P("section", "seq", None),
            P("section", None),
            P("section", "seq", None),
            P("section", "seq", None),
            P("section", "seq", None),
        ),
        out_specs=P("section", "seq", None),
        check_vma=False,
    )
```

profile of v0, /device:TPU:29, one launch (start us, length us, event | category | flops | bytes accessed | tf_op | source)
XLA Modules:
  0.0 441.6 jit_solution(497482587127836714)
XLA Ops:
  6.5 0.0 copy-start
  6.5 0.0 all-gather.2.cloned.1.call-start
  6.5 0.9 mul.186
  7.4 2.1 fusion.17
  9.5 0.0 copy-done
  9.5 2.0 fusion.19
  11.5 0.0 all-gather.2.cloned.1.call-update
  11.5 1.0 copy-done.2
  12.5 0.2 copy.50
  12.7 1.5 broadcast_in_dim.29
  14.3 5.4 %all-to-all-start.1 = ((bf16[512,8,256]{0,2,1:T(8,128)(2,1)}), bf16[512,8,256]{0,2,1:T(8,128)(2,1)S(1)}, u32[]{:S(2)}, u32[]{:S(2)}) async-start(bf16[512,8,256]{0,2,1:T(8,128)(2,1)} %bitcast.11), calls=%async_computation.1 | async-start | bytes 4194304 | tf_op jit(solution)/shard_map/all_to_all | solution.py:93
  19.7 4.2 copy.37
  23.9 4.1 copy.38
  28.0 94.3 %all-to-all-done.1 = bf16[512,8,256]{0,2,1:T(8,128)(2,1)S(1)} async-done(((bf16[512,8,256]{0,2,1:T(8,128)(2,1)}), bf16[512,8,256]{0,2,1:T(8,128)(2,1)S(1)}, u32[]{:S(2)}, u32[]{:S(2)}) %all-to-all-start.1) | async-done | bytes 2097184 | tf_op jit(solution)/shard_map/all_to_all | solution.py:93
  122.3 5.2 %all-to-all-start = ((bf16[512,8,256]{2,0,1:T(8,128)(2,1)}), bf16[512,8,256]{2,0,1:T(8,128)(2,1)}, u32[]{:S(2)}, u32[]{:S(2)}) async-start(bf16[512,8,256]{2,0,1:T(8,128)(2,1)} %copy.38), calls=%async_computation | async-start | bytes 4194304 | tf_op jit(solution)/shard_map/all_to_all | solution.py:92
  127.6 0.0 copy-done.3
  127.6 0.2 copy.51
  127.8 96.9 %all-to-all-done = bf16[512,8,256]{2,0,1:T(8,128)(2,1)} async-done(((bf16[512,8,256]{2,0,1:T(8,128)(2,1)}), bf16[512,8,256]{2,0,1:T(8,128)(2,1)}, u32[]{:S(2)}, u32[]{:S(2)}) %all-to-all-start) | async-done | bytes 2097184 | tf_op jit(solution)/shard_map/all_to_all | solution.py:92
  224.7 1.5 broadcast_in_dim.37
  226.2 7.2 %all-to-all-start.2 = ((bf16[512,8,256]{0,2,1:T(8,128)(2,1)}), bf16[512,8,256]{0,2,1:T(8,128)(2,1)}, u32[]{:S(2)}, u32[]{:S(2)}) async-start(bf16[512,8,256]{0,2,1:T(8,128)(2,1)} %bitcast.17), calls=%async_computation.2 | async-start | bytes 4194304 | tf_op jit(solution)/shard_map/all_to_all | solution.py:94
  233.4 1.9 multiply_cosine_fusion
  235.3 2.5 copy.41
  237.8 2.9 copy.42
  240.7 4.1 copy.39
  244.8 46.2 %all-to-all-done.2 = bf16[512,8,256]{0,2,1:T(8,128)(2,1)} async-done(((bf16[512,8,256]{0,2,1:T(8,128)(2,1)}), bf16[512,8,256]{0,2,1:T(8,128)(2,1)}, u32[]{:S(2)}, u32[]{:S(2)}) %all-to-all-start.2) | async-done | bytes 2097184 | tf_op jit(solution)/shard_map/all_to_all | solution.py:94
  291.1 3.9 copy.44
  295.0 8.3 %fusion.13 = f32[2048,2,128]{0,2,1:T(8,128)S(1)} fusion(bf16[2,128,4096]{2,1,0:T(8,128)(2,1)S(1)} %bitcast.70, bf16[2048,4096]{1,0:T(8,128)(2,1)} %all-gather.2.cloned.1.call-done), kind=kOutput, calls=%fused_computation.18 | convolution fusion | flops 4294967296 | bytes 20971520 | tf_op jit(solution)/shard_map/dot_general | solution.py:102
  303.3 0.0 copy-done.1
  303.3 2.9 copy-done.4
  306.1 4.5 %fusion.15 = f32[2048,2,128]{0,2,1:T(8,128)S(1)} fusion(bf16[2,128,4096]{2,1,0:T(8,128)(2,1)S(1)} %bitcast.71, bf16[2048,4096]{1,0:T(8,128)(2,1)S(1)} %copy-done.4), kind=kOutput, calls=%fused_computation.20 | convolution fusion | flops 4294967296 | bytes 20971520 | tf_op jit(solution)/shard_map/dot_general | solution.py:99
  310.7 0.7 subtract_convert_fusion
  311.4 0.2 pad_maximum_fusion
  311.6 0.9 copy.45
  312.5 11.9 %convolution_convert_fusion = bf16[2048,256]{0,1:T(8,128)(2,1)} fusion(bf16[2048,4096]{1,0:T(8,128)(2,1)} %all-gather.2.cloned.1.call-done, bf16[4096,256]{1,0:T(8,128)(2,1)} %bitcast.69), kind=kOutput, calls=%fused_computation.27 | convolution fusion | flops 4295491584 | bytes 19922944 | tf_op jit(solution)/shard_map/dot_general | solution.py:104
  324.4 53.2 %while.11 = (s32[]{:T(128)}, bf16[4,512,256]{2,1,0:T(8,128)(2,1)}, s32[4]{0:T(128)S(1)}, bf16[2048,256]{0,1:T(8,128)(2,1)S(1)}, bf16[2048,2,128]{2,0,1:T(8,128)(...) while((s32[]{:T(128)}, bf16[4,512,256]{2,1,0:T(8,128)(2,1)}, ...), condition=%wide.region_4.5_spmd.clone, body=%wide.region_1.4_spmd.clone.sunk | while | flops 1087506944 | bytes 23081640 | solution.py:82
  324.4 0.7 dynamic_slice.13
  325.8 0.7 iota_compare_fusion.2
  326.4 5.2 %fusion.38 = (f32[2,512]{1,0:T(2,128)S(1)}, f32[2,512,2048]{2,1,0:T(8,128)}) fusion(pred[512,2048]{1,0:T(8,128)(4,1)S(1)} %iota_compare_fusion.2, bf16[512,2,128]{0,2,1:T(8,128)(2,1)S(1)} %bitcast.63, bf16[2048,2,128]{2,0,1:T(8,128)(2,1)S(1)} %get-tuple-element.176), kind=kOutput, calls=%fused_computation.39.clone.1 | convolution fusion | flops 545261568 | bytes 10752000 | tf_op jit(solution)/shard_map/while/body/eval_jaxpr/sub | solution.py:77
  331.6 5.2 %fusion.39 = bf16[2,512,128]{1,2,0:T(8,128)(2,1)S(1)} fusion(bf16[2048,2,128]{0,2,1:T(8,128)(2,1)} %get-tuple-element.177, f32[2,512,2048]{2,1,0:T(8,128)} %get-tuple-element.150, f32[2,512]{1,0:T(2,128)S(1)} %get-tuple-element.151), kind=kOutput, calls=%fused_computation.11.clone.1 | convolution fusion | flops 541196288 | bytes 9703424 | tf_op jit(solution)/shard_map/while/body/eval_jaxpr/hqk,khd->qhd/dot_general | solution.py:79
  336.8 0.1 copy.55
  337.0 0.7 constant_dynamic-update-slice_fusion.2
  337.7 0.7 dynamic_slice.13
  339.1 0.7 iota_compare_fusion.2
  339.7 5.2 %fusion.38 = (f32[2,512]{1,0:T(2,128)S(1)}, f32[2,512,2048]{2,1,0:T(8,128)}) fusion(pred[512,2048]{1,0:T(8,128)(4,1)S(1)} %iota_compare_fusion.2, bf16[512,2,128]{0,2,1:T(8,128)(2,1)S(1)} %bitcast.63, bf16[2048,2,128]{2,0,1:T(8,128)(2,1)S(1)} %get-tuple-element.176), kind=kOutput, calls=%fused_computation.39.clone.1 | convolution fusion | flops 545261568 | bytes 10752000 | tf_op jit(solution)/shard_map/while/body/eval_jaxpr/sub | solution.py:77
  344.9 5.2 %fusion.39 = bf16[2,512,128]{1,2,0:T(8,128)(2,1)S(1)} fusion(bf16[2048,2,128]{0,2,1:T(8,128)(2,1)} %get-tuple-element.177, f32[2,512,2048]{2,1,0:T(8,128)} %get-tuple-element.150, f32[2,512]{1,0:T(2,128)S(1)} %get-tuple-element.151), kind=kOutput, calls=%fused_computation.11.clone.1 | convolution fusion | flops 541196288 | bytes 9703424 | tf_op jit(solution)/shard_map/while/body/eval_jaxpr/hqk,khd->qhd/dot_general | solution.py:79
  350.1 0.1 copy.55
  350.3 0.7 constant_dynamic-update-slice_fusion.2
  351.0 0.7 dynamic_slice.13
  352.4 0.7 iota_compare_fusion.2
  353.0 5.2 %fusion.38 = (f32[2,512]{1,0:T(2,128)S(1)}, f32[2,512,2048]{2,1,0:T(8,128)}) fusion(pred[512,2048]{1,0:T(8,128)(4,1)S(1)} %iota_compare_fusion.2, bf16[512,2,128]{0,2,1:T(8,128)(2,1)S(1)} %bitcast.63, bf16[2048,2,128]{2,0,1:T(8,128)(2,1)S(1)} %get-tuple-element.176), kind=kOutput, calls=%fused_computation.39.clone.1 | convolution fusion | flops 545261568 | bytes 10752000 | tf_op jit(solution)/shard_map/while/body/eval_jaxpr/sub | solution.py:77
  358.2 5.2 %fusion.39 = bf16[2,512,128]{1,2,0:T(8,128)(2,1)S(1)} fusion(bf16[2048,2,128]{0,2,1:T(8,128)(2,1)} %get-tuple-element.177, f32[2,512,2048]{2,1,0:T(8,128)} %get-tuple-element.150, f32[2,512]{1,0:T(2,128)S(1)} %get-tuple-element.151), kind=kOutput, calls=%fused_computation.11.clone.1 | convolution fusion | flops 541196288 | bytes 9703424 | tf_op jit(solution)/shard_map/while/body/eval_jaxpr/hqk,khd->qhd/dot_general | solution.py:79
  363.4 0.1 copy.55
  363.6 0.7 constant_dynamic-update-slice_fusion.2
  364.3 0.7 dynamic_slice.13
  365.7 0.7 iota_compare_fusion.2
  366.3 5.2 %fusion.38 = (f32[2,512]{1,0:T(2,128)S(1)}, f32[2,512,2048]{2,1,0:T(8,128)}) fusion(pred[512,2048]{1,0:T(8,128)(4,1)S(1)} %iota_compare_fusion.2, bf16[512,2,128]{0,2,1:T(8,128)(2,1)S(1)} %bitcast.63, bf16[2048,2,128]{2,0,1:T(8,128)(2,1)S(1)} %get-tuple-element.176), kind=kOutput, calls=%fused_computation.39.clone.1 | convolution fusion | flops 545261568 | bytes 10752000 | tf_op jit(solution)/shard_map/while/body/eval_jaxpr/sub | solution.py:77
  371.5 5.2 %fusion.39 = bf16[2,512,128]{1,2,0:T(8,128)(2,1)S(1)} fusion(bf16[2048,2,128]{0,2,1:T(8,128)(2,1)} %get-tuple-element.177, f32[2,512,2048]{2,1,0:T(8,128)} %get-tuple-element.150, f32[2,512]{1,0:T(2,128)S(1)} %get-tuple-element.151), kind=kOutput, calls=%fused_computation.11.clone.1 | convolution fusion | flops 541196288 | bytes 9703424 | tf_op jit(solution)/shard_map/while/body/eval_jaxpr/hqk,khd->qhd/dot_general | solution.py:79
  376.7 0.1 copy.55
  376.9 0.7 constant_dynamic-update-slice_fusion.2
  377.6 30.0 %all_to_all.76 = bf16[8,256,256]{2,1,0:T(8,128)(2,1)S(1)} all-to-all(bf16[8,256,256]{2,1,0:T(8,128)(2,1)} %bitcast.72), channel_id=1, replica_groups=mesh['section'=4,'seq'=8] {'seq'}, dimensions={0} | all-to-all | bytes 2097152 | tf_op jit(solution)/shard_map/all_to_all | solution.py:108
  407.6 0.5 copy.47
  408.1 1.3 collective-permute-start
  409.4 24.0 %collective-permute-done = bf16[256,2048]{0,1:T(8,128)(2,1)S(1)} collective-permute-done((bf16[256,2048]{0,1:T(8,128)(2,1)S(1)}, bf16[256,2048]{0,1:T(8,128)(2,1)S(1)}, u32[]{:S(2)}, u32[]{:S(2)}) %collective-permute-start) | collective-permute-done | bytes 1048608 | tf_op jit(solution)/shard_map/ppermute | solution.py:14
  433.4 1.4 copy.48
  (18 shorter events, 0.1 us)
Async XLA Ops:
  6.5 3.0 copy-start
  6.5 288.4 %all-gather.2.cloned.1.call-start = ((), (), s32[]{:S(2)}) async-start(), calls=%async_computation.4 | async-start | bytes 18874368 | tf_op jit(solution)/shard_map/all_gather | solution.py:96
  11.5 1.0 copy-start.2
  14.3 108.1 %all-to-all-start.1 = ((bf16[512,8,256]{0,2,1:T(8,128)(2,1)}), bf16[512,8,256]{0,2,1:T(8,128)(2,1)S(1)}, u32[]{:S(2)}, u32[]{:S(2)}) async-start(bf16[512,8,256]{0,2,1:T(8,128)(2,1)} %bitcast.11), calls=%async_computation.1 | async-start | bytes 4194304 | tf_op jit(solution)/shard_map/all_to_all | solution.py:93
  28.0 99.5 %copy-start.3 = (bf16[1,512,512]{2,1,0:T(8,128)(2,1)S(1)}, bf16[1,512,512]{2,1,0:T(8,128)(2,1)}, u32[]{:S(2)}) copy-start(bf16[1,512,512]{2,1,0:T(8,128)(2,1)} %param.11) | copy-start | bytes 1572868
  122.3 102.3 %all-to-all-start = ((bf16[512,8,256]{2,0,1:T(8,128)(2,1)}), bf16[512,8,256]{2,0,1:T(8,128)(2,1)}, u32[]{:S(2)}, u32[]{:S(2)}) async-start(bf16[512,8,256]{2,0,1:T(8,128)(2,1)} %copy.38), calls=%async_computation | async-start | bytes 4194304 | tf_op jit(solution)/shard_map/all_to_all | solution.py:92
  226.2 64.8 %all-to-all-start.2 = ((bf16[512,8,256]{0,2,1:T(8,128)(2,1)}), bf16[512,8,256]{0,2,1:T(8,128)(2,1)}, u32[]{:S(2)}, u32[]{:S(2)}) async-start(bf16[512,8,256]{0,2,1:T(8,128)(2,1)} %bitcast.17), calls=%async_computation.2 | async-start | bytes 4194304 | tf_op jit(solution)/shard_map/all_to_all | solution.py:94
  295.0 8.3 %copy-start.1 = (bf16[4096,256]{0,1:T(8,128)(2,1)S(1)}, bf16[4096,256]{0,1:T(8,128)(2,1)}, u32[]{:S(2)}) copy-start(bf16[4096,256]{0,1:T(8,128)(2,1)} %copy.39) | copy-start | bytes 6291460
  295.0 11.2 %copy-start.4 = (bf16[2048,4096]{1,0:T(8,128)(2,1)S(1)}, bf16[2048,4096]{1,0:T(8,128)(2,1)}, u32[]{:S(2)}) copy-start(bf16[2048,4096]{1,0:T(8,128)(2,1)} %all-gather.2.cloned.1.call-done) | copy-start | bytes 50331652
  408.1 25.2 %collective-permute-start = (bf16[256,2048]{0,1:T(8,128)(2,1)S(1)}, bf16[256,2048]{0,1:T(8,128)(2,1)S(1)}, u32[]{:S(2)}, u32[]{:S(2)}) collective-permute-start(bf16[256,2048]{0,1:T(8,128)(2,1)S(1)} %bitcast.73), channel_id=1, source_target_pairs={{24,0},{0,8},{8,16},{16,24},{25,1},{1,9},{9,17},{17,25},{26,2},{2,... | collective-permute-start | bytes 3145736 | tf_op jit(solution)/shard_map/ppermute | solution.py:14
Sparse Core Ops, SparseCore 0:
  11.6 269.7 all-gather.1
where the time goes:
time: 446 us; the launch traced here: 442 us
  waiting for transfers between devices  261 us (59%)
  matrix products  66.3 us (15%)
  local copies, waits for them, and re-layouts  38.1 us (9%)
  blocking collectives  30 us (7%)
  starting transfers between devices  19.1 us (4%)
  between operations  13.5 us (3%)
  other arithmetic  10.4 us (2%)
    all_to_all x1, waiting for transfers between devices, per_device(): lax.all_to_all(query_weight, 'seq', split_axis=1, concat_axis=0, tiled=True)  96.9 us
    all_to_all x1, waiting for transfers between devices, per_device(): lax.all_to_all(expand(key_weight), 'seq', split_axis=1, concat_axis=0, ti...  94.3 us
    all_to_all x1, waiting for transfers between devices, per_device(): lax.all_to_all(expand(value_weight), 'seq', split_axis=1, concat_axis=0,...  46.2 us
    all_to_all x1, blocking collectives, per_device(): lax.all_to_all(attended, 'seq', split_axis=0, concat_axis=1, tiled=True)  30 us
    ppermute x1, waiting for transfers between devices, shifted(): return lax.ppermute(block, axis, route)  24 us
    dot_general x4, matrix products, one_block(): jnp.einsum('hqk,khd->qhd', probs, value_heads, preferred_element_type=jnp...  20.8 us
    sub x4, matrix products, one_block(): expon = jnp.exp(scores - maxima)  20.7 us
    dot_general x1, matrix products, per_device(): jnp.dot(gathered, value_cols, preferred_element_type=jnp.float32)  11.9 us
  transfers between devices with their start and end apart: 5, of which 4 were waited for; matrix products, arithmetic and copies ran while one was open for 6% of the time, Pallas kernels for 0%

commit v1 on v0

v1 whole, which is shorter than its diff:
```python
import functools

import jax
import jax.numpy as jnp
from jax import lax
from jax.experimental import pallas as pl
from jax.experimental.pallas import tpu as pltpu
from jax.sharding import PartitionSpec as P

HEAD = 128
LOG2E = 1.4426950408889634


def kernel(
    S, n, hq, group,
    tok_ref, gain_ref, wq_ref, wk_ref, wv_ref, cos_ref, sin_ref, out_ref,
    normed, xbuf, wqb, wkvb, qbuf, kvbuf, sbuf, obuf,
    xrecv, xsend, fsend, gsend, wqrecv, wqsend, wvrecv, wvsend, kvrecv, kvsend, orecv, osend,
):
    s = lax.axis_index("section")
    r = lax.axis_index("seq")
    p, c = r // 2, lax.rem(r, 2)
    v = 2 * s + c
    R = tok_ref.shape[0]
    T = xbuf.shape[0]
    K = xbuf.shape[1]
    piece = R // S
    kb = wq_ref.shape[0]
    qw = hq * HEAD
    prev = lax.rem(s + S - 1, S)
    nxt = lax.rem(p + 1, S)

    def dev(a, b):
        return {"section": a, "seq": b}

    def al(x, m):
        return pl.multiple_of(x, m)

    def post(src, dst, ssem, rsem, a, b):
        is_self = jnp.logical_and(a == s, b == r)

        @pl.when(is_self)
        def _():
            pltpu.make_async_copy(src, dst, rsem).start()

        @pl.when(jnp.logical_not(is_self))
        def _():
            pltpu.make_async_remote_copy(
                src_ref=src, dst_ref=dst, send_sem=ssem, recv_sem=rsem,
                device_id=dev(a, b), device_id_type=pl.DeviceIdType.MESH,
            ).start()

    def sent(src, ssem, a, b):
        @pl.when(jnp.logical_not(jnp.logical_and(a == s, b == r)))
        def _():
            pltpu.make_async_copy(src, src, ssem).wait()

    def arrived(ref, sem):
        pltpu.make_async_copy(ref, ref, sem).wait()

    barrier = pltpu.get_barrier_semaphore()

    def greet(a, b):
        pl.semaphore_signal(
            barrier, inc=1, device_id=dev(a, b), device_id_type=pl.DeviceIdType.MESH
        )

    for b in range(n):
        greet(p, jnp.int32(b))
    for a in range(S):
        for k in range(2):
            greet(jnp.int32(a), 2 * prev + k)
    for d in range(1, S):
        greet(lax.rem(s + d, S), r)
    greet(s, 2 * p + 1 - c)

    gain = gain_ref[...].astype(jnp.float32)

    def norm_step(i, _):
        rows = pl.ds(al(i * 32, 32), 32)
        wide = tok_ref[rows, :].astype(jnp.float32)
        scale = lax.rsqrt(jnp.mean(wide * wide, axis=-1, keepdims=True) + 1e-05)
        normed[rows, :] = (wide * scale * gain).astype(jnp.bfloat16)
        return 0

    lax.fori_loop(0, R // 32, norm_step, 0)
    pl.semaphore_wait(barrier, n + 2 * S + S)

    def xrows(seq, a):
        return xbuf.at[pl.ds(al(seq * R + a * piece, piece), piece), :]

    def first(d):
        a = lax.rem(s + d, S)
        return normed.at[pl.ds(al(a * piece, piece), piece), :], a

    for d in range(S):
        src, a = first(d)
        post(src, xrows(r, a), xsend.at[d], xrecv.at[r * S + a], a, 2 * s + c)

    def wparts(d, k):
        a = lax.rem(s + d, S)
        u = 2 * a + k
        qsrc = wq_ref.at[:, pl.ds(al(u * qw, 128), qw)]
        kvh = (u * hq) // group
        wsrc = (wk_ref, wv_ref)[k].at[:, pl.ds(al(kvh * HEAD, HEAD), HEAD)]
        return a, u, qsrc, wsrc

    krows = pl.ds(al(r * kb, kb), kb)
    for d in range(S):
        for k in range(2):
            a, u, qsrc, wsrc = wparts(d, k)
            post(qsrc, wqb.at[krows, :], wqsend.at[2 * d + k], wqrecv.at[r], a, 2 * s + k)
            post(wsrc, wkvb.at[krows, :], wvsend.at[2 * d + k], wvrecv.at[r], a, 2 * s + k)

    sib = 2 * p + 1 - c

    def relay(t, _):
        j = lax.rem(p + t, S)
        seq = 2 * j + c
        ref = xrows(seq, s)
        sem = xrecv.at[seq * S + s]
        arrived(ref, sem)
        for d in range(1, S):
            post(ref, ref, fsend.at[j * S + d - 1], sem, lax.rem(s + d, S), r)
        post(ref, ref, fsend.at[j * S + S - 1], sem, s, sib)
        return 0

    lax.fori_loop(0, S, relay, 0)

    def relay2(t, _):
        j = lax.rem(p + t, S)
        seq = 2 * j + c
        for d in range(1, S):
            a = lax.rem(s + d, S)
            ref = xrows(seq, a)
            sem = xrecv.at[seq * S + a]
            arrived(ref, sem)
            post(ref, ref, gsend.at[j * S + d - 1], sem, s, sib)
        return 0

    lax.fori_loop(0, S, relay2, 0)

    def gather_w(b, _):
        rows = pl.ds(al(b * kb, kb), kb)
        arrived(wqb.at[rows, :], wqrecv.at[b])
        arrived(wkvb.at[rows, :], wvrecv.at[b])
        return 0

    lax.fori_loop(0, n, gather_w, 0)

    is_k = c == 0

    def kvrows(slot, i):
        return kvbuf.at[slot, pl.ds(al(i * R, R), R), :]

    def project(t, _):
        j = lax.rem(p + t // 2, S)
        other = lax.rem(t, 2)
        i = 2 * j + lax.rem(c + other, 2)

        @pl.when(other == 1)
        def _():
            for a in range(S):
                arrived(xrows(i, a), xrecv.at[i * S + a])

        rows = pl.ds(al(i * R, R), R)
        x = xbuf[rows, :]
        co, si = cos_ref[rows, :], sin_ref[rows, :]
        q = jnp.dot(x, wqb[...], preferred_element_type=jnp.float32)
        for h in range(hq):
            qh = q[:, h * HEAD : (h + 1) * HEAD]
            qbuf[h, rows, :] = (qh * co + pltpu.roll(qh, HEAD // 2, 1) * si).astype(jnp.bfloat16)
        kv = jnp.dot(x, wkvb[...], preferred_element_type=jnp.float32)
        turned = kv * co + pltpu.roll(kv, HEAD // 2, 1) * si
        kvbuf[c, rows, :] = jnp.where(is_k, turned, kv).astype(jnp.bfloat16)
        post(kvrows(c, i), kvrows(c, i), kvsend.at[i], kvrecv.at[i], s, sib)
        return 0

    lax.fori_loop(0, n, project, 0)

    c2 = LOG2E / (HEAD**0.5)

    def oref(i):
        return obuf.at[i]

    ocols = pl.ds(al(v * qw, 128), qw)

    def attend(i, _):
        arrived(kvrows(1 - c, i), kvrecv.at[i])
        rows = pl.ds(al(i * R, R), R)
        for h in range(hq):
            qh = qbuf[h, rows, :]

            def score(t):
                kk = kvbuf[0, pl.ds(al(t * R, R), R), :]
                return lax.dot_general(
                    qh, kk, (((1,), (1,)), ((), ())), preferred_element_type=jnp.float32
                )

            def pass1(t, m):
                sc = score(t)
                sbuf[t] = sc
                return jnp.maximum(m, sc)

            sc = score(i)
            row = lax.broadcasted_iota(jnp.int32, (R, R), 0)
            col = lax.broadcasted_iota(jnp.int32, (R, R), 1)
            sc = jnp.where(col <= row, sc, -jnp.inf)
            sbuf[i] = sc
            m = lax.fori_loop(0, i, pass1, sc)
            top = jnp.max(m, axis=1, keepdims=True)

            def pass2(t, carry):
                acc, tot = carry
                e = jnp.exp2((sbuf[t] - top) * c2)
                vv = kvbuf[1, pl.ds(al(t * R, R), R), :]
                acc = acc + jnp.dot(
                    e.astype(jnp.bfloat16), vv, preferred_element_type=jnp.float32
                )
                return acc, tot + e

            acc, tot = lax.fori_loop(
                0, i + 1, pass2,
                (jnp.zeros((R, HEAD), jnp.float32), jnp.zeros((R, R), jnp.float32)),
            )
            total = jnp.sum(tot, axis=1, keepdims=True)
            obuf[i, :, h * HEAD : (h + 1) * HEAD] = (acc / total).astype(jnp.bfloat16)
        post(oref(i), out_ref.at[:, ocols], osend.at[i], orecv.at[v], nxt, i)
        return 0

    lax.fori_loop(0, n, attend, 0)

    for d in range(S):
        src, a = first(d)
        sent(src, xsend.at[d], a, 2 * s + c)
        for k in range(2):
            a, u, qsrc, wsrc = wparts(d, k)
            sent(wqb.at[krows, :], wqsend.at[2 * d + k], a, 2 * s + k)
            sent(wkvb.at[krows, :], wvsend.at[2 * d + k], a, 2 * s + k)

    def drain(j, _):
        ref = xrows(2 * j + c, s)
        for d in range(S):
            pltpu.make_async_copy(ref, ref, fsend.at[j * S + d]).wait()
        for d in range(1, S):
            o = xrows(2 * j + c, lax.rem(s + d, S))
            pltpu.make_async_copy(o, o, gsend.at[j * S + d - 1]).wait()
        return 0

    lax.fori_loop(0, S, drain, 0)

    def drain_out(i, _):
        pltpu.make_async_copy(kvrows(c, i), kvrows(c, i), kvsend.at[i]).wait()
        sent(oref(i), osend.at[i], nxt, i)
        o = out_ref.at[:, pl.ds(al(i * qw, 128), qw)]
        arrived(o, orecv.at[i])
        return 0

    lax.fori_loop(0, n, drain_out, 0)


def per_device(S, n, tokens, norm_gain, w_query, w_key, w_value):
    R, K = tokens.shape[1:]
    T = R * n
    heads = w_query.shape[2] // HEAD
    hq = heads // n
    group = heads // (w_key.shape[2] // HEAD)
    half = HEAD // 2
    freqs = jnp.power(
        jnp.float32(500000.0), -(jnp.arange(half).astype(jnp.float32) * 2.0 / HEAD)
    )
    angles = jnp.arange(T).astype(jnp.float32)[:, None] * freqs[None, :]
    cosine, sine = jnp.cos(angles), jnp.sin(angles)
    co = jnp.concatenate([cosine, cosine], axis=1)
    si = jnp.concatenate([-sine, sine], axis=1)
    vm = pl.BlockSpec(memory_space=pltpu.VMEM)
    hbm = pl.BlockSpec(memory_space=pl.ANY)
    dma = pltpu.SemaphoreType.DMA
    bf = jnp.bfloat16
    out = pl.pallas_call(
        functools.partial(kernel, S, n, hq, group),
        out_shape=jax.ShapeDtypeStruct((R, heads * HEAD), bf),
        in_specs=[vm, vm, hbm, hbm, hbm, vm, vm],
        out_specs=hbm,
        scratch_shapes=[
            pltpu.VMEM((R, K), bf),
            pltpu.VMEM((T, K), bf),
            pltpu.VMEM((K, hq * HEAD), bf),
            pltpu.VMEM((K, HEAD), bf),
            pltpu.VMEM((hq, T, HEAD), bf),
            pltpu.VMEM((2, T, HEAD), bf),
            pltpu.VMEM((n, R, R), jnp.float32),
            pltpu.VMEM((n, R, hq * HEAD), bf),
            dma((n * S,)), dma((S,)), dma((S * S,)), dma((S * S,)),
            dma((n,)), dma((n,)), dma((n,)), dma((n,)),
            dma((n,)), dma((n,)), dma((n,)), dma((n,)),
        ],
        compiler_params=pltpu.CompilerParams(
            collective_id=0, has_side_effects=True, vmem_limit_bytes=60 * 1024 * 1024
        ),
    )(tokens[0], norm_gain, w_query[0], w_key[0], w_value[0], co, si)
    return out[None]


def solution(mesh):
    S, n = mesh.shape["section"], mesh.shape["seq"]
    spec = P("section", "seq", None)
    return jax.shard_map(
        functools.partial(per_device, S, n),
        mesh=mesh,
        in_specs=(spec, P("section", None), spec, spec, spec),
        out_specs=spec,
        check_vma=False,
    )
```

time: 446 us -> 432 us (0.969)
  the two profiles are of different devices: /device:TPU:29 before, /device:TPU:27 now
where the time goes in v1:
time: 432 us
  Pallas kernels  424 us (98%)
  other arithmetic  5.67 us (1%)
    pallas_call x1, Pallas kernels, per_device(): pl.pallas_call(functools.partial(kernel, S, n, hq, group), out_shape=jax....  424 us

profile of v1, /device:TPU:27, one launch (start us, length us, event | category | flops | bytes accessed | tf_op | source)
XLA Modules:
  0.0 431.8 jit_solution(2807317748047958510)
XLA Ops:
  0.0 3.7 fusion
  3.7 1.9 pad_maximum_fusion
  5.7 423.8 %shard_map.55 = bf16[256,2048]{1,0:T(8,128)(2,1)} custom-call(bf16[256,4096]{1,0:T(8,128)(2,1)} %bitcast.6, bf16[1,4096]{1,0:T(2,128)(2,1)} %gain_ref.1, bf16[512,2048]{1,0:T(8,128)(2,1)} %bitcast.7, bf16[512,512]{1,0:T(8,128)(2,1)} %bitcast.8, bf16[512,512]{1,0:T(8,128)(2,1)} %bitcast.9, f32[2048,128]{1,0:T(8,128)} %get-tuple-element.8.cos_ref, ...), custom_call_target="tpu_custom_call" | custom-call | tf_op jit(solution)/shard_map/pallas_call | solution.py:280
  429.4 2.3 copy.7
  (2 shorter events, 0.0 us)

commit v2 on v1

--- a/solution.py
+++ b/solution.py
@@ -14,8 +14,8 @@
 def kernel(
     S, n, hq, group,
     tok_ref, gain_ref, wq_ref, wk_ref, wv_ref, cos_ref, sin_ref, out_ref,
-    normed, xbuf, wqb, wkvb, qbuf, kvbuf, sbuf, obuf,
-    xrecv, xsend, fsend, gsend, wqrecv, wqsend, wvrecv, wvsend, kvrecv, kvsend, orecv, osend,
+    normed, xbuf, wqb, wkvb, qbuf, kvbuf, sbuf, obuf, xst, wsq, wsk, wsv,
+    xsr, wsr, wss, xz, xrecv, xsend, fsend, gsend, wqrecv, wqsend, wvrecv, wvsend, kvrecv, kvsend, orecv, osend,
 ):
     s = lax.axis_index("section")
     r = lax.axis_index("seq")
@@ -66,13 +66,12 @@
         )
 
     for b in range(n):
-        greet(p, jnp.int32(b))
+        greet(s, jnp.int32(b))
     for a in range(S):
         for k in range(2):
             greet(jnp.int32(a), 2 * prev + k)
-    for d in range(1, S):
+    for d in range(S):
         greet(lax.rem(s + d, S), r)
-    greet(s, 2 * p + 1 - c)
 
     gain = gain_ref[...].astype(jnp.float32)
 
@@ -84,7 +83,7 @@
         return 0
 
     lax.fori_loop(0, R // 32, norm_step, 0)
-    pl.semaphore_wait(barrier, n + 2 * S + S)
+    pl.semaphore_wait(barrier, 2 * n + S)
 
     def xrows(seq, a):
         return xbuf.at[pl.ds(al(seq * R + a * piece, piece), piece), :]
@@ -95,22 +94,48 @@
 
     for d in range(S):
         src, a = first(d)
-        post(src, xrows(r, a), xsend.at[d], xrecv.at[r * S + a], a, 2 * s + c)
-
-    def wparts(d, k):
+        post(src, xst.at[s], xsend.at[d], xsr.at[s], a, r)
+
+    def wfirst(d):
         a = lax.rem(s + d, S)
-        u = 2 * a + k
-        qsrc = wq_ref.at[:, pl.ds(al(u * qw, 128), qw)]
-        kvh = (u * hq) // group
-        wsrc = (wk_ref, wv_ref)[k].at[:, pl.ds(al(kvh * HEAD, HEAD), HEAD)]
-        return a, u, qsrc, wsrc
+        head = pl.ds(al(((2 * a * hq) // group) * HEAD, HEAD), HEAD)
+        return a, (
+            (wq_ref.at[:, pl.ds(al(2 * a * qw, 128), 2 * qw)], wsq.at[s]),
+            (wk_ref.at[:, head], wsk.at[s]),
+            (wv_ref.at[:, head], wsv.at[s]),
+        )
+
+    for d in range(S):
+        a, parts = wfirst(d)
+        for k, (src, dst) in enumerate(parts):
+            post(src, dst, wss.at[k, d], wsr.at[k, s], a, r)
 
     krows = pl.ds(al(r * kb, kb), kb)
-    for d in range(S):
+
+    def second_x(t, _):
+        j = lax.rem(p + 1 + t, S)
+        arrived(xst.at[j], xsr.at[j])
+        post(xst.at[j], xrows(r, s), xz.at[j], xrecv.at[r * S + s], s, 2 * j + c)
+        return 0
+
+    lax.fori_loop(0, S, second_x, 0)
+
+    def second_w(t, _):
+        j = lax.rem(p + 1 + t, S)
+        for k, buf in enumerate((wsq, wsk, wsv)):
+            arrived(buf.at[j], wsr.at[k, j])
         for k in range(2):
-            a, u, qsrc, wsrc = wparts(d, k)
-            post(qsrc, wqb.at[krows, :], wqsend.at[2 * d + k], wqrecv.at[r], a, 2 * s + k)
-            post(wsrc, wkvb.at[krows, :], wvsend.at[2 * d + k], wvrecv.at[r], a, 2 * s + k)
+            post(
+                wsq.at[j, :, k * qw : (k + 1) * qw], wqb.at[krows, :],
+                wqsend.at[2 * j + k], wqrecv.at[r], s, 2 * j + k,
+            )
+            post(
+                (wsk, wsv)[k].at[j], wkvb.at[krows, :],
+                wvsend.at[2 * j + k], wvrecv.at[r], s, 2 * j + k,
+            )
+        return 0
+
+    lax.fori_loop(0, S, second_w, 0)
 
     sib = 2 * p + 1 - c
 
@@ -232,13 +257,16 @@
 
     for d in range(S):
         src, a = first(d)
-        sent(src, xsend.at[d], a, 2 * s + c)
+        sent(src, xsend.at[d], a, r)
+        a, parts = wfirst(d)
+        for k, (_, dst) in enumerate(parts):
+            sent(dst, wss.at[k, d], a, r)
+
+    def drain(j, _):
+        sent(xst.at[j], xz.at[j], s, 2 * j + c)
         for k in range(2):
-            a, u, qsrc, wsrc = wparts(d, k)
-            sent(wqb.at[krows, :], wqsend.at[2 * d + k], a, 2 * s + k)
-            sent(wkvb.at[krows, :], wvsend.at[2 * d + k], a, 2 * s + k)
-
-    def drain(j, _):
+            sent(wqb.at[krows, :], wqsend.at[2 * j + k], s, 2 * j + k)
+            sent(wkvb.at[krows, :], wvsend.at[2 * j + k], s, 2 * j + k)
         ref = xrows(2 * j + c, s)
         for d in range(S):
             pltpu.make_async_copy(ref, ref, fsend.at[j * S + d]).wait()
@@ -291,6 +319,11 @@
             pltpu.VMEM((2, T, HEAD), bf),
             pltpu.VMEM((n, R, R), jnp.float32),
             pltpu.VMEM((n, R, hq * HEAD), bf),
+            pltpu.VMEM((S, R // S, K), bf),
+            pltpu.VMEM((S, K // n, 2 * hq * HEAD), bf),
+            pltpu.VMEM((S, K // n, HEAD), bf),
+            pltpu.VMEM((S, K // n, HEAD), bf),
+            dma((S,)), dma((3, S)), dma((3, S)), dma((S,)),
             dma((n * S,)), dma((S,)), dma((S * S,)), dma((S * S,)),
             dma((n,)), dma((n,)), dma((n,)), dma((n,)),
             dma((n,)), dma((n,)), dma((n,)), dma((n,)),

time: 432 us -> 255 us (0.59)
  the two profiles are of different devices: /device:TPU:27 before, /device:TPU:29 now
where the time goes in v2:
time: 255 us
  Pallas kernels  247 us (97%)
  other arithmetic  5.67 us (2%)
    pallas_call x1, Pallas kernels, per_device(): pl.pallas_call(functools.partial(kernel, S, n, hq, group), out_shape=jax....  247 us

profile of v2, /device:TPU:29, one launch (start us, length us, event | category | flops | bytes accessed | tf_op | source)
XLA Modules:
  0.0 255.1 jit_solution(3518171105548444797)
XLA Ops:
  0.0 3.7 %fusion = (f32[2048,64]{1,0:T(8,128)S(1)}, f32[2048,64]{1,0:T(8,128)S(1)}, f32[2048,64]{1,0:T(8,128)S(1)}) fusion(f32[64]{0:T(128)S(1)} %negate_power_fusion, f32[2048]{0:T(1024)S(1)} %iota_convert_fusion), kind=kLoop, calls=%fused_computation.4 | loop fusion | flops 262144 | bytes 1581312 | tf_op jit(solution)/shard_map/neg | solution.py:303
  3.7 1.9 pad_maximum_fusion
  5.7 247.1 %shard_map.55 = bf16[256,2048]{1,0:T(8,128)(2,1)} custom-call(bf16[256,4096]{1,0:T(8,128)(2,1)} %bitcast.6, bf16[1,4096]{1,0:T(2,128)(2,1)} %gain_ref.1, bf16[512,2048]{1,0:T(8,128)(2,1)} %bitcast.7, bf16[512,512]{1,0:T(8,128)(2,1)} %bitcast.8, bf16[512,512]{1,0:T(8,128)(2,1)} %bitcast.9, f32[2048,128]{1,0:T(8,128)} %get-tuple-element.8.cos_ref, ...), custom_call_target="tpu_custom_call" | custom-call | tf_op jit(solution)/shard_map/pallas_call | solution.py:308
  252.8 2.3 copy.7
  (2 shorter events, 0.0 us)

commit v3 on v2

--- a/solution.py
+++ b/solution.py
@@ -139,8 +139,7 @@
 
     sib = 2 * p + 1 - c
 
-    def relay(t, _):
-        j = lax.rem(p + t, S)
+    def relay(j, _):
         seq = 2 * j + c
         ref = xrows(seq, s)
         sem = xrecv.at[seq * S + s]
@@ -152,8 +151,7 @@
 
     lax.fori_loop(0, S, relay, 0)
 
-    def relay2(t, _):
-        j = lax.rem(p + t, S)
+    def relay2(j, _):
         seq = 2 * j + c
         for d in range(1, S):
             a = lax.rem(s + d, S)
@@ -163,7 +161,7 @@
             post(ref, ref, gsend.at[j * S + d - 1], sem, s, sib)
         return 0
 
-    lax.fori_loop(0, S, relay2, 0)
+    relay2(0, 0)
 
     def gather_w(b, _):
         rows = pl.ds(al(b * kb, kb), kb)
@@ -179,7 +177,7 @@
         return kvbuf.at[slot, pl.ds(al(i * R, R), R), :]
 
     def project(t, _):
-        j = lax.rem(p + t // 2, S)
+        j = t // 2
         other = lax.rem(t, 2)
         i = 2 * j + lax.rem(c + other, 2)
 
@@ -201,8 +199,6 @@
         post(kvrows(c, i), kvrows(c, i), kvsend.at[i], kvrecv.at[i], s, sib)
         return 0
 
-    lax.fori_loop(0, n, project, 0)
-
     c2 = LOG2E / (HEAD**0.5)
 
     def oref(i):
@@ -253,7 +249,13 @@
         post(oref(i), out_ref.at[:, ocols], osend.at[i], orecv.at[v], nxt, i)
         return 0
 
-    lax.fori_loop(0, n, attend, 0)
+    def stage(j, _):
+        lax.fori_loop(jnp.maximum(j, 1), j + 1, relay2, 0)
+        lax.fori_loop(2 * j, 2 * j + 2, project, 0)
+        lax.fori_loop(2 * j, 2 * j + 2, attend, 0)
+        return 0
+
+    lax.fori_loop(0, S, stage, 0)
 
     for d in range(S):
         src, a = first(d)

time: 255 us -> 219 us (0.86)
  Pallas kernels: 247 us -> 211 us
    pallas_call x1, Pallas kernels: 247 us -> 211 us  [per_device(): pl.pallas_call(functools.partial(kernel, S, n, hq, group), out_shape=jax....]
where the time goes in v3:
time: 219 us
  Pallas kernels  211 us (96%)
  other arithmetic  5.67 us (3%)
  local copies, waits for them, and re-layouts  2.3 us (1%)
    pallas_call x1, Pallas kernels, per_device(): pl.pallas_call(functools.partial(kernel, S, n, hq, group), out_shape=jax....  211 us

profile of v3, /device:TPU:29, one launch (start us, length us, event | category | flops | bytes accessed | tf_op | source)
XLA Modules:
  0.0 218.8 jit_solution(1754114038554696143)
XLA Ops:
  0.0 3.7 %fusion = (f32[2048,64]{1,0:T(8,128)S(1)}, f32[2048,64]{1,0:T(8,128)S(1)}, f32[2048,64]{1,0:T(8,128)S(1)}) fusion(f32[64]{0:T(128)S(1)} %negate_power_fusion, f32[2048]{0:T(1024)S(1)} %iota_convert_fusion), kind=kLoop, calls=%fused_computation.4 | loop fusion | flops 262144 | bytes 1581312 | tf_op jit(solution)/shard_map/neg | solution.py:305
  3.7 1.9 pad_maximum_fusion
  5.7 210.8 %shard_map.55 = bf16[256,2048]{1,0:T(8,128)(2,1)} custom-call(bf16[256,4096]{1,0:T(8,128)(2,1)} %bitcast.6, bf16[1,4096]{1,0:T(2,128)(2,1)} %gain_ref.1, bf16[512,2048]{1,0:T(8,128)(2,1)} %bitcast.7, bf16[512,512]{1,0:T(8,128)(2,1)} %bitcast.8, bf16[512,512]{1,0:T(8,128)(2,1)} %bitcast.9, f32[2048,128]{1,0:T(8,128)} %get-tuple-element.8.cos_ref, ...), custom_call_target="tpu_custom_call" | custom-call | tf_op jit(solution)/shard_map/pallas_call | solution.py:310
  216.5 2.3 %copy.7 = bf16[1,256,2048]{2,1,0:T(8,128)(2,1)} copy(bf16[1,256,2048]{2,1,0:T(8,128)(2,1)} %bitcast.5) | data formatting | bytes 2097152
  (2 shorter events, 0.0 us)

commit v4 on v3

--- a/solution.py
+++ b/solution.py
@@ -135,8 +135,6 @@
             )
         return 0
 
-    lax.fori_loop(0, S, second_w, 0)
-
     sib = 2 * p + 1 - c
 
     def relay(j, _):
@@ -149,7 +147,12 @@
         post(ref, ref, fsend.at[j * S + S - 1], sem, s, sib)
         return 0
 
-    lax.fori_loop(0, S, relay, 0)
+    def hops(t, _):
+        relay(t, 0)
+        second_w(t, 0)
+        return 0
+
+    lax.fori_loop(0, S, hops, 0)
 
     def relay2(j, _):
         seq = 2 * j + c

time: 219 us -> 221 us (level)
  no operation moved by 1% of the time
where the time goes in v4:
time: 221 us
  Pallas kernels  213 us (96%)
  other arithmetic  5.67 us (3%)
  local copies, waits for them, and re-layouts  2.3 us (1%)
    pallas_call x1, Pallas kernels, per_device(): pl.pallas_call(functools.partial(kernel, S, n, hq, group), out_shape=jax....  213 us

profile of v4, /device:TPU:29, one launch (start us, length us, event | category | flops | bytes accessed | tf_op | source)
XLA Modules:
  0.0 220.6 jit_solution(1107157287724362032)
XLA Ops:
  0.0 3.7 %fusion = (f32[2048,64]{1,0:T(8,128)S(1)}, f32[2048,64]{1,0:T(8,128)S(1)}, f32[2048,64]{1,0:T(8,128)S(1)}) fusion(f32[64]{0:T(128)S(1)} %negate_power_fusion, f32[2048]{0:T(1024)S(1)} %iota_convert_fusion), kind=kLoop, calls=%fused_computation.4 | loop fusion | flops 262144 | bytes 1581312 | tf_op jit(solution)/shard_map/neg | solution.py:308
  3.7 1.9 pad_maximum_fusion
  5.7 212.6 %shard_map.55 = bf16[256,2048]{1,0:T(8,128)(2,1)} custom-call(bf16[256,4096]{1,0:T(8,128)(2,1)} %bitcast.6, bf16[1,4096]{1,0:T(2,128)(2,1)} %gain_ref.1, bf16[512,2048]{1,0:T(8,128)(2,1)} %bitcast.7, bf16[512,512]{1,0:T(8,128)(2,1)} %bitcast.8, bf16[512,512]{1,0:T(8,128)(2,1)} %bitcast.9, f32[2048,128]{1,0:T(8,128)} %get-tuple-element.8.cos_ref, ...), custom_call_target="tpu_custom_call" | custom-call | tf_op jit(solution)/shard_map/pallas_call | solution.py:313
  218.3 2.3 %copy.7 = bf16[1,256,2048]{2,1,0:T(8,128)(2,1)} copy(bf16[1,256,2048]{2,1,0:T(8,128)(2,1)} %bitcast.5) | data formatting | bytes 2097152
  (2 shorter events, 0.0 us)

commit v5 on v3

--- a/solution.py
+++ b/solution.py
@@ -209,41 +209,50 @@
     def attend(i, _):
         arrived(kvrows(1 - c, i), kvrecv.at[i])
         rows = pl.ds(al(i * R, R), R)
-        for h in range(hq):
-            qh = qbuf[h, rows, :]
-
-            def score(t):
-                kk = kvbuf[0, pl.ds(al(t * R, R), R), :]
-                return lax.dot_general(
-                    qh, kk, (((1,), (1,)), ((), ())), preferred_element_type=jnp.float32
-                )
-
-            def pass1(t, m):
-                sc = score(t)
-                sbuf[t] = sc
-                return jnp.maximum(m, sc)
-
-            sc = score(i)
-            row = lax.broadcasted_iota(jnp.int32, (R, R), 0)
-            col = lax.broadcasted_iota(jnp.int32, (R, R), 1)
-            sc = jnp.where(col <= row, sc, -jnp.inf)
-            sbuf[i] = sc
-            m = lax.fori_loop(0, i, pass1, sc)
-            top = jnp.max(m, axis=1, keepdims=True)
-
-            def pass2(t, carry):
-                acc, tot = carry
-                e = jnp.exp2((sbuf[t] - top) * c2)
-                vv = kvbuf[1, pl.ds(al(t * R, R), R), :]
+        heads = range(hq)
+
+        def fold(op, x):
+            parts = [x[:, k : k + HEAD] for k in range(0, R, HEAD)]
+            return functools.reduce(op, parts)
+
+        def score(h, t):
+            return lax.dot_general(
+                qbuf[h, rows, :], kvbuf[0, pl.ds(al(t * R, R), R), :],
+                (((1,), (1,)), ((), ())), preferred_element_type=jnp.float32,
+            )
+
+        def pass1(t, ms):
+            scs = [score(h, t) for h in heads]
+            for h in heads:
+                sbuf[h, t] = scs[h]
+            return tuple(jnp.maximum(ms[h], fold(jnp.maximum, scs[h])) for h in heads)
+
+        row = lax.broadcasted_iota(jnp.int32, (R, R), 0)
+        col = lax.broadcasted_iota(jnp.int32, (R, R), 1)
+        first_max = []
+        for h in heads:
+            sc = jnp.where(col <= row, score(h, i), -jnp.inf)
+            sbuf[h, i] = sc
+            first_max.append(fold(jnp.maximum, sc))
+        ms = lax.fori_loop(0, i, pass1, tuple(first_max))
+        tops = [jnp.max(m, axis=1, keepdims=True) for m in ms]
+
+        def pass2(t, carry):
+            vv = kvbuf[1, pl.ds(al(t * R, R), R), :]
+            new = []
+            for h in heads:
+                acc, tot = carry[h]
+                e = jnp.exp2((sbuf[h, t] - tops[h]) * c2)
                 acc = acc + jnp.dot(
                     e.astype(jnp.bfloat16), vv, preferred_element_type=jnp.float32
                 )
-                return acc, tot + e
-
-            acc, tot = lax.fori_loop(
-                0, i + 1, pass2,
-                (jnp.zeros((R, HEAD), jnp.float32), jnp.zeros((R, R), jnp.float32)),
-            )
+                new.append((acc, tot + fold(jnp.add, e)))
+            return tuple(new)
+
+        zero = jnp.zeros((R, HEAD), jnp.float32)
+        sums = lax.fori_loop(0, i + 1, pass2, tuple((zero, zero) for _ in heads))
+        for h in heads:
+            acc, tot = sums[h]
             total = jnp.sum(tot, axis=1, keepdims=True)
             obuf[i, :, h * HEAD : (h + 1) * HEAD] = (acc / total).astype(jnp.bfloat16)
         post(oref(i), out_ref.at[:, ocols], osend.at[i], orecv.at[v], nxt, i)
@@ -319,7 +328,7 @@
             pltpu.VMEM((K, HEAD), bf),
             pltpu.VMEM((hq, T, HEAD), bf),
             pltpu.VMEM((2, T, HEAD), bf),
-            pltpu.VMEM((n, R, R), jnp.float32),
+            pltpu.VMEM((hq, n, R, R), jnp.float32),
             pltpu.VMEM((n, R, hq * HEAD), bf),
             pltpu.VMEM((S, R // S, K), bf),
             pltpu.VMEM((S, K // n, 2 * hq * HEAD), bf),

time: 219 us -> 210 us (0.959)
  Pallas kernels: 211 us -> 200 us
    pallas_call x1, Pallas kernels: 211 us -> 200 us  [per_device(): pl.pallas_call(functools.partial(kernel, S, n, hq, group), out_shape=jax....]
where the time goes in v5:
time: 210 us; the launch traced here: 208 us
  Pallas kernels  200 us (95%)
  other arithmetic  5.67 us (3%)
  local copies, waits for them, and re-layouts  2.3 us (1%)
    pallas_call x1, Pallas kernels, per_device(): pl.pallas_call(functools.partial(kernel, S, n, hq, group), out_shape=jax....  200 us

profile of v5, /device:TPU:29, one launch (start us, length us, event | category | flops | bytes accessed | tf_op | source)
XLA Modules:
  0.0 207.9 jit_solution(529528111679994721)
XLA Ops:
  0.0 3.7 %fusion = (f32[2048,64]{1,0:T(8,128)S(1)}, f32[2048,64]{1,0:T(8,128)S(1)}, f32[2048,64]{1,0:T(8,128)S(1)}) fusion(f32[64]{0:T(128)S(1)} %negate_power_fusion, f32[2048]{0:T(1024)S(1)} %iota_convert_fusion), kind=kLoop, calls=%fused_computation.4 | loop fusion | flops 262144 | bytes 1581312 | tf_op jit(solution)/shard_map/neg | solution.py:314
  3.7 1.9 pad_maximum_fusion
  5.7 199.9 %shard_map.55 = bf16[256,2048]{1,0:T(8,128)(2,1)} custom-call(bf16[256,4096]{1,0:T(8,128)(2,1)} %bitcast.6, bf16[1,4096]{1,0:T(2,128)(2,1)} %gain_ref.1, bf16[512,2048]{1,0:T(8,128)(2,1)} %bitcast.7, bf16[512,512]{1,0:T(8,128)(2,1)} %bitcast.8, bf16[512,512]{1,0:T(8,128)(2,1)} %bitcast.9, f32[2048,128]{1,0:T(8,128)} %get-tuple-element.8.cos_ref, ...), custom_call_target="tpu_custom_call" | custom-call | tf_op jit(solution)/shard_map/pallas_call | solution.py:319
  205.6 2.3 %copy.7 = bf16[1,256,2048]{2,1,0:T(8,128)(2,1)} copy(bf16[1,256,2048]{2,1,0:T(8,128)(2,1)} %bitcast.5) | data formatting | bytes 2097152
  (2 shorter events, 0.0 us)
